TPU v7x, 32 devices: a whole 2x2x4 slice. The times are simulated.
32 devices in a mesh: group: 2 (over x), rows: 16 (over z, y, core).
Axes of the slice: x: 2, y: 2, z: 4, core: 2. Of those that a mesh axis runs over, the one named last changes fastest.
Arguments:
- spectra: float32 [4, 1024, 6144], P('group', 'rows'), parts along dimension 0, may hold values from -6 to 6
- plane: float32 [1024, 6144], P('rows'), may hold values from -6 to 6
- interval_edges: int32 [12, 2], replicated, may hold values from 0 to 128
- tile_shifts: int32 [4, 12, 2], P('group'), parts along dimension 0, may hold values from -8 to 8, as said below
Outputs:
- correlation: float32 [4, 1024, 6144], P('group', 'rows'), parts along dimension 0
- aligned_spectra: float32 [4, 1024, 6144], P('group', 'rows'), parts along dimension 0
There are 2 independent parts, one for each index of `group`. A program takes and returns all parts, laid end to end along the dimension named above; an argument that names none is the same for every part. Nothing has to cross between parts.
Inputs may be any that keep to these rules, and one draw needn't show every extreme that they name: `tile_shifts`: both shifts lie in -8 to 8; the 1024 shift equals 8 for some tile and -8 for another in every draw.
All inputs are finite; a program needn't handle non-finite values.
Results may differ from a plain program's by a relative error of at most 0.000098.
Values sent between devices are 32-bit elements; how exact they have to be, the bound alone decides.
A program may use at most 128 MiB of HBM per device.

v0:
```python
import math

import jax
import jax.numpy as jnp
import numpy as np
from jax import lax
from jax.experimental import pallas as pl
from jax.experimental.pallas import tpu as pltpu
from jax.sharding import PartitionSpec as P

F1 = 1024
TF2 = 512
HALF = TF2 // 2
MAXS = 8
LANES = 128

exact = lax.Precision.HIGH
full = lax.Precision.HIGHEST


def trig(rows, columns, modulus):
    angle = np.outer(np.arange(rows), np.arange(columns)) % modulus * (2.0 * math.pi / modulus)
    return np.cos(angle), np.sin(angle)


def column_table():
    return np.stack(trig(F1, F1, F1))


def row_tables(span):
    groups = HALF // span
    cosine, sine = trig(TF2, HALF, TF2)
    alternate = np.where(np.arange(TF2) % 2 == 0, 1.0, -1.0)
    forward_imag = -sine
    forward_imag[:, 0] = alternate
    forward = np.stack([cosine, forward_imag], axis=1)
    forward = forward.reshape(TF2, 2, groups, span).transpose(0, 2, 1, 3)
    forward = forward.reshape(TF2, groups, 2 * span)
    weights = np.where(np.arange(HALF) == 0, 1.0, 2.0)[None, :]
    inverse_imag = -2.0 * sine
    inverse_imag[:, 0] = alternate
    inverse = np.stack([weights * cosine, inverse_imag], axis=1)
    inverse = inverse.reshape(TF2, 2, groups, span).transpose(2, 1, 3, 0)
    inverse = inverse.reshape(groups, 2 * span, TF2) * float(F1 * TF2) ** (-1.5)
    return forward.astype(np.float32), inverse.astype(np.float32)


def align_kernel(shifts, body, above, below, out, padded):
    spectrum = pl.program_id(0)
    height, breadth = body.shape[1:]
    total = height + 2 * MAXS
    margin = jnp.zeros((total, LANES), jnp.float32)
    padded[:, :LANES] = margin
    padded[:, LANES + breadth :] = margin
    padded[:MAXS, LANES : LANES + breadth] = above[0]
    padded[MAXS : MAXS + height, LANES : LANES + breadth] = body[0]
    padded[MAXS + height :, LANES : LANES + breadth] = below[0]
    window = TF2 + 2 * LANES
    for tile in range(breadth // TF2):
        down = shifts[spectrum, tile, 0]
        right = shifts[spectrum, tile, 1]
        part = padded[:, tile * TF2 : tile * TF2 + window]
        part = pltpu.roll(part, lax.rem(right + window, window), 1)[:, LANES : LANES + TF2]
        part = pltpu.roll(part, lax.rem(down + total, total), 0)
        out[0, :, tile * TF2 : (tile + 1) * TF2] = part[MAXS : MAXS + height]


def aligned(spectra, tile_shifts):
    number, height, breadth = spectra.shape
    count = lax.axis_size("rows")
    head = spectra[:, :MAXS]
    tail = spectra[:, height - MAXS :]
    above = lax.ppermute(tail, "rows", [(i, i + 1) for i in range(count - 1)])
    below = lax.ppermute(head, "rows", [(i + 1, i) for i in range(count - 1)])
    whole = pl.BlockSpec((1, height, breadth), lambda s: (s, 0, 0))
    edge = pl.BlockSpec((1, MAXS, breadth), lambda s: (s, 0, 0))
    return pl.pallas_call(
        align_kernel,
        grid=(number,),
        out_shape=jax.ShapeDtypeStruct(spectra.shape, jnp.float32),
        in_specs=[pl.BlockSpec(memory_space=pltpu.SMEM), whole, edge, edge],
        out_specs=whole,
        scratch_shapes=[pltpu.VMEM((height + 2 * MAXS, breadth + 2 * LANES), jnp.float32)],
        compiler_params=pltpu.CompilerParams(vmem_limit_bytes=24 * 2**20),
        cost_estimate=pl.CostEstimate(
            flops=20 * spectra.size, bytes_accessed=8 * spectra.size, transcendentals=0
        ),
    )(tile_shifts, spectra, above, below)


def plain_products(plane_columns, received, packed):
    count, local, height, width = plane_columns.shape
    span = width // 2
    columns = column_table().astype(np.float32)

    def halves(block):
        pencil = block.transpose(0, 2, 1, 3).reshape(F1, local * width)
        both = jnp.einsum("pkn,nl->pkl", columns, pencil, precision=exact)
        return both.reshape(2, F1, local, 2, span)

    def spectrum_of(both):
        cosine, sine = both[0], both[1]
        return cosine[:, :, 0] + sine[:, :, 1], cosine[:, :, 1] - sine[:, :, 0]

    plane_halves = halves(plane_columns)
    plane_real, plane_imag = spectrum_of(plane_halves)

    def back(block):
        both = halves(block)
        real, imag = spectrum_of(both)
        out_real = real * plane_real + imag * plane_imag
        out_imag = imag * plane_real - real * plane_imag
        cosine, sine = both[0], both[1]
        pc, ps = plane_halves[0], plane_halves[1]
        mask = packed[None, :, None, :]
        first = jnp.stack([out_real, out_imag], axis=2)
        second = jnp.stack([-out_imag, out_real], axis=2)
        first = jnp.where(mask, cosine * pc + sine * ps, first)
        second = jnp.where(mask, sine * pc - cosine * ps, second)
        pair = jnp.stack([first, second]).reshape(2, F1, local * width)
        rows = jnp.einsum("pkn,pnl->kl", columns, pair, precision=exact)
        return rows.reshape(count, height, local, width).transpose(0, 2, 1, 3)

    return [back(block) for block in received]


def split(values):
    high = values.astype(jnp.bfloat16)
    return high, (values - high.astype(jnp.float32)).astype(jnp.bfloat16)


def product_3(table_high, table_low, rows, high, low):
    def dot(a, b):
        return jnp.dot(a, b, preferred_element_type=jnp.float32)

    top = table_high[rows, :]
    return dot(top, high) + (dot(top, low) + dot(table_low[rows, :], high))


CHUNK = 256


def forward_halves(table_high, table_low, block, both, high, low):
    count, local, height, width = block.shape
    for source in range(count):
        for part in range(local):
            rows = slice(source * height, (source + 1) * height)
            lanes = slice(part * width, (part + 1) * width)
            high[rows, lanes], low[rows, lanes] = split(block[source, part])

    @pl.loop(0, 2 * F1 // CHUNK)
    def _(step):
        rows = pl.ds(pl.multiple_of(step * CHUNK, CHUNK), CHUNK)
        both[rows, :] = product_3(table_high, table_low, rows, high[...], low[...])


def product_kernel(
    table_high, table_low, block, plane_both, packed, out, both, high, low, pair_high, pair_low
):
    count, local, height, width = block.shape
    forward_halves(table_high, table_low, block, both, high, low)
    rows_per = 64
    lane = lax.broadcasted_iota(jnp.int32, (rows_per, width), 1)
    is_real = lane < width // 2
    sign = jnp.where(is_real, 1.0, -1.0).astype(jnp.float32)

    def swap(values):
        return pltpu.roll(values, width // 2, 1)

    @pl.loop(0, F1 // rows_per)
    def _(step):
        top = pl.ds(pl.multiple_of(step * rows_per, rows_per), rows_per)
        bottom = pl.ds(pl.multiple_of(F1 + step * rows_per, rows_per), rows_per)
        for part in range(local):
            lanes = slice(part * width, (part + 1) * width)
            c, s = both[top, lanes], both[bottom, lanes]
            pc, ps = plane_both[top, lanes], plane_both[bottom, lanes]
            value = c + sign * swap(s)
            plane_value = pc + sign * swap(ps)
            same = value * plane_value
            cross = swap(value) * plane_value
            product = jnp.where(is_real, same + swap(same), swap(cross) - cross)
            alone = packed[0:1, lanes] > 0.5
            first = jnp.where(alone, c * pc + s * ps, product)
            second = jnp.where(alone, s * pc - c * ps, -sign * swap(product))
            pair_high[top, lanes], pair_low[top, lanes] = split(first)
            pair_high[bottom, lanes], pair_low[bottom, lanes] = split(second)

    per_step = CHUNK // height

    @pl.loop(0, F1 // CHUNK)
    def _(step):
        total = jnp.zeros((CHUNK, local * width), jnp.float32)
        for side in range(2):
            rows = pl.ds(pl.multiple_of(side * F1 + step * CHUNK, CHUNK), CHUNK)
            own = slice(side * F1, (side + 1) * F1)
            total += product_3(table_high, table_low, rows, pair_high[own], pair_low[own])
        for place in range(per_step):
            for part in range(local):
                out[step * per_step + place, part] = total[
                    place * height : (place + 1) * height, part * width : (part + 1) * width
                ]


def kernel_products(plane_columns, received, packed):
    count, local, height, width = plane_columns.shape
    breadth = local * width
    table = column_table().reshape(2 * F1, F1)
    table_high = table.astype(jnp.bfloat16)
    table_low = (table - table_high.astype(np.float64)).astype(jnp.bfloat16)
    lanes = jnp.stack([packed, packed], axis=1).reshape(1, breadth).astype(jnp.float32)
    flops = 12 * F1 * F1 * breadth
    space = pl.BlockSpec(memory_space=pltpu.VMEM)
    params = pltpu.CompilerParams(vmem_limit_bytes=44 * 2**20)
    halves_shape = (2 * F1, breadth)
    scratch = [pltpu.VMEM((F1, breadth), jnp.bfloat16)] * 2
    plane_both = pl.pallas_call(
        forward_halves,
        out_shape=jax.ShapeDtypeStruct(halves_shape, jnp.float32),
        in_specs=[space] * 3,
        out_specs=space,
        scratch_shapes=scratch,
        compiler_params=params,
        cost_estimate=pl.CostEstimate(
            flops=flops, bytes_accessed=8 * F1 * F1, transcendentals=0
        ),
    )(table_high, table_low, plane_columns)
    call = pl.pallas_call(
        product_kernel,
        out_shape=jax.ShapeDtypeStruct(plane_columns.shape, jnp.float32),
        in_specs=[space] * 5,
        out_specs=space,
        scratch_shapes=[pltpu.VMEM(halves_shape, jnp.float32)]
        + scratch
        + [pltpu.VMEM(halves_shape, jnp.bfloat16)] * 2,
        compiler_params=params,
        cost_estimate=pl.CostEstimate(
            flops=2 * flops, bytes_accessed=8 * F1 * F1, transcendentals=0
        ),
    )
    return [call(table_high, table_low, block, plane_both, lanes) for block in received]


def per_device(spectra, plane, interval_edges, tile_shifts):
    number, height, breadth = spectra.shape
    count = lax.axis_size("rows")
    tiles = breadth // TF2
    span = math.gcd(breadth // 2 // count, HALF)
    groups = HALF // span
    width = 2 * span
    local = tiles * groups // count
    forward, inverse = row_tables(span)

    point = jnp.arange(TF2, dtype=jnp.int32)[None, :]
    inside = (point >= interval_edges[:, 0:1]) & (point < TF2 - interval_edges[:, 1:2])
    keeper = jnp.where(inside, 1.0, 0.0).astype(jnp.float32).reshape(1, breadth)

    def to_columns(rows):
        blocks = rows.reshape(height, tiles, TF2)
        bins = jnp.einsum("rbn,njl->bjrl", blocks, forward, precision=full)
        sent = bins.reshape(count, local, height, width)
        return lax.all_to_all(sent, "rows", split_axis=0, concat_axis=0, tiled=True)

    granule = lax.axis_index("rows") * local + jnp.arange(local, dtype=jnp.int32)
    packed = (granule % groups == 0)[:, None] & (jnp.arange(span) == 0)[None, :]
    plane_columns = to_columns(plane)
    received = [to_columns(spectra[s] * keeper) for s in range(number)]
    aligned_spectra = aligned(spectra, tile_shifts)
    if width == LANES and height % 16 == 0:
        products = kernel_products(plane_columns, received, packed)
    else:
        products = plain_products(plane_columns, received, packed)
    returned = [
        lax.all_to_all(block, "rows", split_axis=0, concat_axis=0, tiled=True)
        for block in products
    ]

    def to_rows(block):
        bins = block.reshape(tiles, groups, height, width)
        return jnp.einsum("bjrl,jln->rbn", bins, inverse, precision=full).reshape(height, breadth)

    correlation = jnp.stack([to_rows(block) for block in returned])
    return (correlation, aligned_spectra)


def solution(mesh):
    placed = (P("group", "rows", None), P("rows", None), P(), P("group", None, None))
    return jax.shard_map(
        per_device,
        mesh=mesh,
        in_specs=placed,
        out_specs=(P("group", "rows", None), P("group", "rows", None)),
        check_vma=False,
    )
```

profile of v0, /device:TPU:15, one launch (start us, length us, event | category | flops | bytes accessed | tf_op | source)
XLA Modules:
  0.0 257.5 jit_solution(9462021325858507153)
XLA Ops:
  0.6 0.8 slice_bitcast_fusion
  1.4 3.8 %fusion.12 = (f32[1,64,6144]{2,1,0:T(8,128)}, f32[1,64,6144]{2,1,0:T(8,128)}) fusion(f32[2,64,6144]{2,1,0:T(8,128)} %body.1), kind=kLoop, calls=%fused_computation.28 | loop fusion | bytes 6291456 | tf_op jit(solution)/shard_map/slice | solution.py:267
  5.2 1.7 squeeze.6
  7.0 2.8 %squeeze.7 = f32[64,12,512]{2,1,0:T(8,128)} reshape(f32[1,64,6144]{2,1,0:T(8,128)} %get-tuple-element.5) | data formatting | bytes 3145728 | tf_op jit(solution)/shard_map/squeeze | solution.py:267
  9.8 0.1 fusion.8
  9.9 0.0 copy-start.10
  9.9 3.5 %multiply_bitcast_fusion.1 = (f32[64,12,512,1]{2,1,0,3:T(8,128)S(1)}, f32[64,12,512,1]{2,1,0,3:T(8,128)}) fusion(f32[64,12,512]{2,1,0:T(8,128)S(1)} %squeeze.6, f32[12,512]{1,0:T(8,128)S(1)} %fusion.8, f32[64,12,512]{2,1,0:T(8,128)} %squeeze.7), kind=kLoop, calls=%fused_computation.2 | loop fusion | flops 786432 | bytes 6316032 | tf_op jit(solution)/shard_map/mul | solution.py:267
  13.4 0.0 copy-done.10
  13.4 4.6 %fusion.4 = f32[64,12,4,128]{3,0,2,1:T(8,128)} fusion(f32[512,4,128,1]{2,0,1,3:T(8,128)S(1)} %copy-done.10, f32[64,12,512,1]{2,1,0,3:T(8,128)S(1)} %get-tuple-element.6), kind=kOutput, calls=%fused_computation.8 | convolution fusion | flops 2415919104 | bytes 4194304 | tf_op jit(solution)/shard_map/rbn,njl->bjrl/dot_general | solution.py:260
  18.0 0.0 copy-start.11
  18.0 6.7 %all-to-all-start = ((f32[16,3,64,128]{3,2,1,0:T(8,128)}), f32[16,3,64,128]{3,2,1,0:T(8,128)S(1)}, u32[]{:S(2)}, u32[]{:S(2)}) async-start(f32[16,3,64,128]{3,2,1,0:T(8,128)} %bitcast.5), calls=%async_computation | async-start | bytes 3145728 | tf_op jit(solution)/shard_map/all_to_all | solution.py:262
  24.7 0.0 copy-done.11
  24.7 3.9 %fusion.6 = f32[12,4,64,128]{3,2,0,1:T(8,128)S(1)} fusion(f32[512,4,128,1]{2,0,3,1:T(8,128)} %constant.41, f32[8,12,8,512]{3,2,1,0:T(8,128)S(1)} %bitcast.53), kind=kOutput, calls=%fused_computation.10 | convolution fusion | flops 2415919104 | bytes 4194304 | tf_op jit(solution)/shard_map/rbn,njl->bjrl/dot_general | solution.py:260
  28.6 1.4 copy.20
  29.9 30.9 %all-to-all-done.block = f32[16,3,64,128]{3,2,1,0:T(8,128)S(1)} async-done(((f32[16,3,64,128]{3,2,1,0:T(8,128)}), f32[16,3,64,128]{3,2,1,0:T(8,128)S(1)}, u32[]{:S(2)}, u32[]{:S(2)}) %all-to-all-start) | async-done | bytes 1572896 | tf_op jit(solution)/shard_map/all_to_all | solution.py:262
  60.8 4.9 %all-to-all-start.1 = ((f32[16,3,64,128]{3,2,1,0:T(8,128)}), f32[16,3,64,128]{3,2,1,0:T(8,128)S(1)}, u32[]{:S(2)}, u32[]{:S(2)}) async-start(f32[16,3,64,128]{3,2,1,0:T(8,128)} %bitcast.51), calls=%async_computation.1 | async-start | bytes 3145728 | tf_op jit(solution)/shard_map/all_to_all | solution.py:262
  65.7 6.4 %fusion.2 = f32[64,12,4,128]{3,0,2,1:T(8,128)} fusion(f32[512,4,128,1]{2,0,1,3:T(8,128)} %constant.40, f32[64,12,512,1]{2,1,0,3:T(8,128)} %get-tuple-element.7), kind=kOutput, calls=%fused_computation.6 | convolution fusion | flops 2415919104 | bytes 4194304 | tf_op jit(solution)/shard_map/rbn,njl->bjrl/dot_general | solution.py:260
  72.2 29.8 %all-to-all-done.1.block = f32[16,3,64,128]{3,2,1,0:T(8,128)S(1)} async-done(((f32[16,3,64,128]{3,2,1,0:T(8,128)}), f32[16,3,64,128]{3,2,1,0:T(8,128)S(1)}, u32[]{:S(2)}, u32[]{:S(2)}) %all-to-all-start.1) | async-done | bytes 1572896 | tf_op jit(solution)/shard_map/all_to_all | solution.py:262
  101.9 0.0 copy-start.2
  101.9 1.1 copy-done.2
  103.1 4.9 %all-to-all-start.3 = ((f32[16,3,64,128]{3,2,1,0:T(8,128)}), f32[16,3,64,128]{3,2,1,0:T(8,128)S(1)}, u32[]{:S(2)}, u32[]{:S(2)}) async-start(f32[16,3,64,128]{3,2,1,0:T(8,128)} %bitcast.52), calls=%async_computation.3 | async-start | bytes 3145728 | tf_op jit(solution)/shard_map/all_to_all | solution.py:262
  108.0 0.1 broadcast_and_fusion
  108.1 0.1 reshape.141.packed
  108.2 0.0 copy-start.3
  108.2 1.4 copy-done.3
  109.6 0.0 copy-start.5
  109.6 2.2 copy-done.5
  111.8 10.3 %shard_map.122.plane_both = f32[2048,384]{1,0:T(8,128)S(1)} custom-call(bf16[2048,1024]{1,0:T(8,128)(2,1)S(1)} %copy-done.5, bf16[2048,1024]{1,0:T(8,128)(2,1)} %constant.38.clone.table_low, f32[16,3,64,128]{3,2,1,0:T(8,128)S(1)} %copy-done.3), custom_call_target="tpu_custom_call" | custom-call | flops 4831838208 | bytes 8388608 | tf_op jit(solution)/shard_map/pallas_call | solution.py:217
  122.1 23.8 %shard_map.123 = f32[16,3,64,128]{3,2,1,0:T(8,128)S(1)} custom-call(bf16[2048,1024]{1,0:T(8,128)(2,1)} %constant.37.clone.table_high, bf16[2048,1024]{1,0:T(8,128)(2,1)} %constant.38.clone.table_low, f32[16,3,64,128]{3,2,1,0:T(8,128)S(1)} %all-to-all-done.block, f32[2048,384]{1,0:T(8,128)S(1)} %shard_map.122.plane_both, f32[1,384]{1,0:T(1,128)S(1)} %reshape.141.packed), custom_call_target="tpu_custom_call" | custom-call | flops 9663676416 | bytes 8388608 | tf_op jit(solution)/shard_map/pallas_call | solution.py:241
  145.9 0.0 copy-start.4
  145.9 1.1 copy-done.4
  147.0 0.0 copy-start.6
  147.0 1.7 copy-done.6
  148.7 0.0 all-to-all-done.3.block
  148.7 6.0 %all-to-all-start.2 = ((f32[16,3,64,128]{3,2,1,0:T(8,128)}), f32[16,3,64,128]{3,2,1,0:T(8,128)}, u32[]{:S(2)}, u32[]{:S(2)}) async-start(f32[16,3,64,128]{3,2,1,0:T(8,128)} %copy-done.4), calls=%async_computation.2 | async-start | bytes 3145728 | tf_op jit(solution)/shard_map/all_to_all | solution.py:274
  154.7 0.0 copy-start.7
  154.7 1.9 copy-done.7
  156.6 23.8 %shard_map.124 = f32[16,3,64,128]{3,2,1,0:T(8,128)S(1)} custom-call(bf16[2048,1024]{1,0:T(8,128)(2,1)} %constant.37.clone.table_high, bf16[2048,1024]{1,0:T(8,128)(2,1)} %constant.38.clone.table_low, f32[16,3,64,128]{3,2,1,0:T(8,128)S(1)} %all-to-all-done.3.block, f32[2048,384]{1,0:T(8,128)S(1)} %copy-done.7, f32[1,384]{1,0:T(1,128)S(1)} %reshape.141.packed), custom_call_target="tpu_custom_call" | custom-call | flops 9663676416 | bytes 8388608 | tf_op jit(solution)/shard_map/pallas_call | solution.py:241
  180.4 0.0 copy-start.1
  180.4 1.1 copy-done.1
  181.6 0.0 copy-start
  181.6 9.5 %all-to-all-done.2 = f32[16,3,64,128]{3,2,1,0:T(8,128)} async-done(((f32[16,3,64,128]{3,2,1,0:T(8,128)}), f32[16,3,64,128]{3,2,1,0:T(8,128)}, u32[]{:S(2)}, u32[]{:S(2)}) %all-to-all-start.2) | async-done | bytes 1572896 | tf_op jit(solution)/shard_map/all_to_all | solution.py:274
  191.0 4.9 %all-to-all-start.4 = ((f32[16,3,64,128]{3,2,1,0:T(8,128)}), f32[16,3,64,128]{3,2,1,0:T(8,128)}, u32[]{:S(2)}, u32[]{:S(2)}) async-start(f32[16,3,64,128]{3,2,1,0:T(8,128)} %copy-done.1), calls=%async_computation.4 | async-start | bytes 3145728 | tf_op jit(solution)/shard_map/all_to_all | solution.py:274
  195.9 0.0 copy-done
  195.9 0.9 fusion.11
  196.9 3.3 %collective-permute-start = (f32[2,8,6144]{2,1,0:T(8,128)}, f32[2,8,6144]{2,1,0:T(8,128)S(1)}, u32[]{:S(2)}, u32[]{:S(2)}) collective-permute-start(f32[2,8,6144]{2,1,0:T(8,128)} %get-tuple-element.3), channel_id=1, source_target_pairs={{0,1},{1,2},{2,3},{3,4},{4,5},{5,6},{6,7},{7,8},{8,9},{9,10},{10,1... | collective-permute-start | bytes 1179656 | tf_op jit(solution)/shard_map/ppermute | solution.py:73
  200.2 2.1 collective-permute-start.1
  202.3 0.8 copy.24.shifts
  203.1 0.0 copy-start.8
  203.1 31.6 %collective-permute-done.above = f32[2,8,6144]{2,1,0:T(8,128)S(1)} collective-permute-done((f32[2,8,6144]{2,1,0:T(8,128)}, f32[2,8,6144]{2,1,0:T(8,128)S(1)}, u32[]{:S(2)}, u32[]{:S(2)}) %collective-permute-start) | collective-permute-done | bytes 393248 | tf_op jit(solution)/shard_map/ppermute | solution.py:73
  234.8 1.6 collective-permute-done.1.below
  236.3 4.1 %shard_map.125 = f32[2,64,6144]{2,1,0:T(8,128)} custom-call(s32[2,12,2]{2,1,0:T(8,128)S(1)} %copy.24.shifts, f32[2,64,6144]{2,1,0:T(8,128)S(1)} %copy-done, f32[2,8,6144]{2,1,0:T(8,128)S(1)} %collective-permute-done.above, f32[2,8,6144]{2,1,0:T(8,128)} %collective-permute-done.1.below), custom_call_target="tpu_custom_call" | custom-call | flops 15728640 | bytes 6291456 | tf_op jit(solution)/shard_map/pallas_call | solution.py:77
  240.5 0.0 copy-done.8
  240.5 4.0 %convolution_bitcast_fusion.1 = f32[64,12,512]{2,0,1:T(8,128)S(1)} fusion(f32[12,4,64,128]{3,2,1,0:T(8,128)} %bitcast.10, f32[4,128,512,1]{2,1,0,3:T(8,128)S(1)} %copy-done.8), kind=kOutput, calls=%fused_computation.12 | convolution fusion | flops 2415919104 | bytes 4194304 | tf_op jit(solution)/shard_map/bjrl,jln->rbn/dot_general | solution.py:280
  244.5 0.9 copy.21
  245.5 0.0 copy-start.9
  245.5 1.6 stack_reshape.6
  247.1 0.0 all-to-all-done.4
  247.1 0.0 copy-done.9
  247.1 4.0 %convolution_bitcast_fusion = f32[64,12,512]{2,0,1:T(8,128)S(1)} fusion(f32[12,4,64,128]{3,2,1,0:T(8,128)} %bitcast.18, f32[4,128,512,1]{2,1,0,3:T(8,128)S(1)} %copy-done.9), kind=kOutput, calls=%fused_computation.11 | convolution fusion | flops 2415919104 | bytes 4194304 | tf_op jit(solution)/shard_map/bjrl,jln->rbn/dot_general | solution.py:280
  251.2 0.9 copy.23
  252.1 1.6 stack_reshape.7
  253.7 3.8 %pad_maximum_fusion = f32[2,64,6144]{2,1,0:T(8,128)} fusion(f32[1,64,6144]{2,1,0:T(8,128)} %stack_reshape.7, f32[1,64,6144]{2,1,0:T(8,128)} %stack_reshape.6), kind=kLoop, calls=%fused_computation | loop fusion | flops 786432 | bytes 6291456 | tf_op jit(solution)/shard_map/stack | solution.py:282
  (3 shorter events, 0.0 us)
Async XLA Ops:
  9.9 3.5 %copy-start.10 = (f32[512,4,128,1]{2,0,1,3:T(8,128)S(1)}, f32[512,4,128,1]{2,0,1,3:T(8,128)}, u32[]{:S(2)}) copy-start(f32[512,4,128,1]{2,0,1,3:T(8,128)} %constant.40) | copy-start | bytes 3145732
  18.0 6.7 %copy-start.11 = (f32[64,6144]{1,0:T(8,128)S(1)}, f32[64,6144]{1,0:T(8,128)}, u32[]{:S(2)}) copy-start(f32[64,6144]{1,0:T(8,128)} %param.12) | copy-start | bytes 4718596
  18.0 42.9 %all-to-all-start = ((f32[16,3,64,128]{3,2,1,0:T(8,128)}), f32[16,3,64,128]{3,2,1,0:T(8,128)S(1)}, u32[]{:S(2)}, u32[]{:S(2)}) async-start(f32[16,3,64,128]{3,2,1,0:T(8,128)} %bitcast.5), calls=%async_computation | async-start | bytes 3145728 | tf_op jit(solution)/shard_map/all_to_all | solution.py:262
  60.8 41.1 %all-to-all-start.1 = ((f32[16,3,64,128]{3,2,1,0:T(8,128)}), f32[16,3,64,128]{3,2,1,0:T(8,128)S(1)}, u32[]{:S(2)}, u32[]{:S(2)}) async-start(f32[16,3,64,128]{3,2,1,0:T(8,128)} %bitcast.51), calls=%async_computation.1 | async-start | bytes 3145728 | tf_op jit(solution)/shard_map/all_to_all | solution.py:262
  101.9 1.1 copy-start.2
  103.1 45.6 %all-to-all-start.3 = ((f32[16,3,64,128]{3,2,1,0:T(8,128)}), f32[16,3,64,128]{3,2,1,0:T(8,128)S(1)}, u32[]{:S(2)}, u32[]{:S(2)}) async-start(f32[16,3,64,128]{3,2,1,0:T(8,128)} %bitcast.52), calls=%async_computation.3 | async-start | bytes 3145728 | tf_op jit(solution)/shard_map/all_to_all | solution.py:262
  108.2 1.4 copy-start.3
  109.6 2.2 copy-start.5
  145.9 1.2 copy-start.4
  147.0 1.7 copy-start.6
  148.7 42.3 %all-to-all-start.2 = ((f32[16,3,64,128]{3,2,1,0:T(8,128)}), f32[16,3,64,128]{3,2,1,0:T(8,128)}, u32[]{:S(2)}, u32[]{:S(2)}) async-start(f32[16,3,64,128]{3,2,1,0:T(8,128)} %copy-done.4), calls=%async_computation.2 | async-start | bytes 3145728 | tf_op jit(solution)/shard_map/all_to_all | solution.py:274
  154.7 1.9 copy-start.7
  180.4 1.1 copy-start.1
  181.6 14.4 %copy-start = (f32[2,64,6144]{2,1,0:T(8,128)S(1)}, f32[2,64,6144]{2,1,0:T(8,128)}, u32[]{:S(2)}) copy-start(f32[2,64,6144]{2,1,0:T(8,128)} %body.1) | copy-start | bytes 9437188
  191.0 56.1 %all-to-all-start.4 = ((f32[16,3,64,128]{3,2,1,0:T(8,128)}), f32[16,3,64,128]{3,2,1,0:T(8,128)}, u32[]{:S(2)}, u32[]{:S(2)}) async-start(f32[16,3,64,128]{3,2,1,0:T(8,128)} %copy-done.1), calls=%async_computation.4 | async-start | bytes 3145728 | tf_op jit(solution)/shard_map/all_to_all | solution.py:274
  196.9 37.9 %collective-permute-start = (f32[2,8,6144]{2,1,0:T(8,128)}, f32[2,8,6144]{2,1,0:T(8,128)S(1)}, u32[]{:S(2)}, u32[]{:S(2)}) collective-permute-start(f32[2,8,6144]{2,1,0:T(8,128)} %get-tuple-element.3), channel_id=1, source_target_pairs={{0,1},{1,2},{2,3},{3,4},{4,5},{5,6},{6,7},{7,8},{8,9},{9,10},{10,1... | collective-permute-start | bytes 1179656 | tf_op jit(solution)/shard_map/ppermute | solution.py:73
  200.2 36.1 %collective-permute-start.1 = (f32[2,8,6144]{2,1,0:T(8,128)}, f32[2,8,6144]{2,1,0:T(8,128)}, u32[]{:S(2)}, u32[]{:S(2)}) collective-permute-start(f32[2,8,6144]{2,1,0:T(8,128)} %get-tuple-element.2), channel_id=1, source_target_pairs={{1,0},{2,1},{3,2},{4,3},{5,4},{6,5},{7,6},{8,7},{9,8},{10,9},{11,1... | collective-permute-start | bytes 1179656 | tf_op jit(solution)/shard_map/ppermute | solution.py:74
  203.1 37.4 %copy-start.8 = (f32[4,128,512,1]{2,1,0,3:T(8,128)S(1)}, f32[4,128,512,1]{2,1,0,3:T(8,128)}, u32[]{:S(2)}) copy-start(f32[4,128,512,1]{2,1,0,3:T(8,128)} %constant.42) | copy-start | bytes 3145732
  245.5 1.6 copy-start.9
where the time goes:
time: 258 us
  waiting for transfers between devices  103 us (40%)
  Pallas kernels  62 us (24%)
  starting transfers between devices  32.9 us (13%)
  local copies, waits for them, and re-layouts  27.3 us (11%)
  matrix products  23 us (9%)
  other arithmetic  8.29 us (3%)
    all_to_all x3, waiting for transfers between devices, to_columns(): return lax.all_to_all(sent, 'rows', split_axis=0, concat_axis=0, tiled=True)  60.7 us
    pallas_call x2, Pallas kernels, kernel_products(): call(table_high, table_low, block, plane_both, lanes)  47.6 us
    ppermute x1, waiting for transfers between devices, aligned(): above = lax.ppermute(tail, 'rows', [(i, i + 1) for i in range(count - 1)])  31.6 us
    all_to_all x3, starting transfers between devices, to_columns(): return lax.all_to_all(sent, 'rows', split_axis=0, concat_axis=0, tiled=True)  16.5 us
    dot_general x3, matrix products, to_columns(): bins = jnp.einsum('rbn,njl->bjrl', blocks, forward, precision=full)  14.9 us
    unnamed x25, local copies, waits for them, and re-layouts  11.4 us
    all_to_all x2, starting transfers between devices, per_device(): lax.all_to_all(block, 'rows', split_axis=0, concat_axis=0, tiled=True)  10.9 us
    pallas_call x1, Pallas kernels, kernel_products(): pl.pallas_call(forward_halves, out_shape=jax.ShapeDtypeStruct(halves_shap...  10.3 us
  transfers between devices with their start and end apart: 7, of which 5 were waited for; matrix products, arithmetic and copies ran while one was open for 8% of the time, Pallas kernels for 24%

commit v1 on v0

--- a/solution.py
+++ b/solution.py
@@ -42,7 +42,7 @@
     inverse = np.stack([weights * cosine, inverse_imag], axis=1)
     inverse = inverse.reshape(TF2, 2, groups, span).transpose(2, 1, 3, 0)
     inverse = inverse.reshape(groups, 2 * span, TF2) * float(F1 * TF2) ** (-1.5)
-    return forward.astype(np.float32), inverse.astype(np.float32)
+    return forward, inverse
 
 
 def align_kernel(shifts, body, above, below, out, padded):
@@ -241,6 +241,72 @@
     return [call(table_high, table_low, block, plane_both, lanes) for block in received]
 
 
+def product_of(values, table_high, table_low):
+    high, low = split(values)
+
+    def dot(a, b):
+        return jnp.dot(a, b, preferred_element_type=jnp.float32)
+
+    return dot(high, table_high) + (dot(low, table_high) + dot(high, table_low))
+
+
+def bins_kernel(keeper, rows, table_high, table_low, out):
+    bins = product_of(rows[...] * keeper[...], table_high[...], table_low[...])
+    for group in range(out.shape[0]):
+        out[group] = bins[:, group * LANES : (group + 1) * LANES]
+
+
+def rows_kernel(*refs):
+    blocks, (table_high, table_low, out) = refs[:-3], refs[-3:]
+    for spectrum, block in enumerate(blocks):
+        bins = jnp.concatenate([block[group] for group in range(block.shape[0])], axis=1)
+        out[spectrum] = product_of(bins, table_high[...], table_low[...])
+
+
+def split_table(table):
+    high = table.astype(jnp.bfloat16)
+    return high, (table - high.astype(np.float64)).astype(jnp.bfloat16)
+
+
+def kernel_bins(spectra, index, keeper, table):
+    height, breadth = spectra.shape[1:]
+    tiles, groups = breadth // TF2, TF2 // LANES
+    fixed = pl.BlockSpec((TF2, TF2), lambda b: (0, 0))
+    return pl.pallas_call(
+        bins_kernel,
+        grid=(tiles,),
+        out_shape=jax.ShapeDtypeStruct((tiles * groups, height, LANES), jnp.float32),
+        in_specs=[
+            pl.BlockSpec((1, TF2), lambda b: (0, b)),
+            pl.BlockSpec((None, height, TF2), lambda b: (index, 0, b)),
+            fixed,
+            fixed,
+        ],
+        out_specs=pl.BlockSpec((groups, height, LANES), lambda b: (b, 0, 0)),
+        compiler_params=pltpu.CompilerParams(vmem_limit_bytes=24 * 2**20),
+        cost_estimate=pl.CostEstimate(
+            flops=6 * height * breadth * TF2, bytes_accessed=8 * height * breadth, transcendentals=0
+        ),
+    )(keeper, spectra, *split_table(table))
+
+
+def kernel_rows(blocks, table):
+    granules, height = blocks[0].shape[:2]
+    groups = TF2 // LANES
+    tiles = granules // groups
+    number = len(blocks)
+    fixed = pl.BlockSpec((TF2, TF2), lambda b: (0, 0))
+    return pl.pallas_call(
+        rows_kernel,
+        grid=(tiles,),
+        out_shape=jax.ShapeDtypeStruct((number, height, tiles * TF2), jnp.float32),
+        in_specs=[pl.BlockSpec((groups, height, LANES), lambda b: (b, 0, 0))] * number
+        + [fixed, fixed],
+        out_specs=pl.BlockSpec((number, height, TF2), lambda b: (0, 0, b)),
+        compiler_params=pltpu.CompilerParams(vmem_limit_bytes=24 * 2**20),
+    )(*blocks, *split_table(table))
+
+
 def per_device(spectra, plane, interval_edges, tile_shifts):
     number, height, breadth = spectra.shape
     count = lax.axis_size("rows")
@@ -255,18 +321,35 @@
     inside = (point >= interval_edges[:, 0:1]) & (point < TF2 - interval_edges[:, 1:2])
     keeper = jnp.where(inside, 1.0, 0.0).astype(jnp.float32).reshape(1, breadth)
 
-    def to_columns(rows):
-        blocks = rows.reshape(height, tiles, TF2)
-        bins = jnp.einsum("rbn,njl->bjrl", blocks, forward, precision=full)
-        sent = bins.reshape(count, local, height, width)
+    cohorts = lax.axis_size("group")
+    share = height // cohorts
+    whole_tiles = width == LANES and share % 16 == 0
+
+    def to_columns(rows, index, kept):
+        held = rows.shape[1]
+        if whole_tiles:
+            bins = kernel_bins(rows, index, kept, forward.reshape(TF2, TF2))
+        else:
+            blocks = (rows[index] * kept).reshape(held, tiles, TF2)
+            table = forward.astype(np.float32)
+            bins = jnp.einsum("rbn,njl->bjrl", blocks, table, precision=full)
+        sent = bins.reshape(count, local, held, width)
         return lax.all_to_all(sent, "rows", split_axis=0, concat_axis=0, tiled=True)
 
     granule = lax.axis_index("rows") * local + jnp.arange(local, dtype=jnp.int32)
     packed = (granule % groups == 0)[:, None] & (jnp.arange(span) == 0)[None, :]
-    plane_columns = to_columns(plane)
-    received = [to_columns(spectra[s] * keeper) for s in range(number)]
+    own = lax.axis_index("group")
+    plane_rows = lax.dynamic_slice_in_dim(plane, own * share, share, axis=0)
+    mine = to_columns(plane_rows[None], 0, jnp.ones_like(keeper))
+    if cohorts == 2:
+        other = lax.ppermute(mine, "group", [(0, 1), (1, 0)])
+        ordered = [jnp.where(own == 0, mine, other), jnp.where(own == 0, other, mine)]
+        plane_columns = jnp.concatenate(ordered, axis=2)
+    else:
+        plane_columns = lax.all_gather(mine, "group", axis=2, tiled=True)
+    received = [to_columns(spectra, s, keeper) for s in range(number)]
     aligned_spectra = aligned(spectra, tile_shifts)
-    if width == LANES and height % 16 == 0:
+    if whole_tiles:
         products = kernel_products(plane_columns, received, packed)
     else:
         products = plain_products(plane_columns, received, packed)
@@ -275,9 +358,14 @@
         for block in products
     ]
 
+    if whole_tiles:
+        blocks = [block.reshape(tiles * groups, height, width) for block in returned]
+        return (kernel_rows(blocks, inverse.reshape(TF2, TF2)), aligned_spectra)
+
     def to_rows(block):
         bins = block.reshape(tiles, groups, height, width)
-        return jnp.einsum("bjrl,jln->rbn", bins, inverse, precision=full).reshape(height, breadth)
+        table = inverse.astype(np.float32)
+        return jnp.einsum("bjrl,jln->rbn", bins, table, precision=full).reshape(height, breadth)
 
     correlation = jnp.stack([to_rows(block) for block in returned])
     return (correlation, aligned_spectra)

time: 258 us -> 251 us (0.973)
  Pallas kernels: 62 us -> 93.7 us
  matrix products: 23 us -> 0 us
  other arithmetic: 8.29 us -> 2.04 us
  waiting for transfers between devices: 103 us -> 97.1 us
  local copies, waits for them, and re-layouts: 27.3 us -> 22.5 us
    pallas_call x0 -> x4, Pallas kernels: none -> 31.3 us  [the longest x3 19.9 us: kernel_bins(): pl.pallas_call(bins_kernel, grid=(tiles,), out_shape=jax.ShapeDtypeStruct...]
    dot_general x5 -> x0, matrix products: 23 us -> none  [the longest x3 14.9 us: to_columns(): bins = jnp.einsum('rbn,njl->bjrl', blocks, forward, precision=full)]
    all_to_all x3, waiting for transfers between devices: 60.7 us -> 38.2 us  [to_columns(): return lax.all_to_all(sent, 'rows', split_axis=0, concat_axis=0, tiled=True)]
    ppermute x0 -> x1, waiting for transfers between devices: none -> 18.6 us  [per_device(): other = lax.ppermute(mine, 'group', [(0, 1), (1, 0)])]
    unnamed x25 -> x36, local copies, waits for them, and re-layouts: 11.4 us -> 20.3 us
    squeeze x2 -> x0, local copies, waits for them, and re-layouts: 4.58 us -> none  [per_device(): received = [to_columns(spectra[s] * keeper) for s in range(number)]]
    another operation x1 -> x0, other arithmetic: 3.85 us -> none  [per_device(): correlation = jnp.stack([to_rows(block) for block in returned])]
    slice x1 -> x0, local copies, waits for them, and re-layouts: 3.84 us -> none  [per_device(): received = [to_columns(spectra[s] * keeper) for s in range(number)]]
  transfers between devices with their start and end apart: 7 -> 8, of which waited for: 5 -> 6; matrix products, arithmetic and copies ran while one was open for 8% -> 2% of each run, Pallas kernels for 24% -> 30%
where the time goes in v1:
time: 251 us; the launch traced here: 250 us
  waiting for transfers between devices  97.1 us (39%)
  Pallas kernels  93.7 us (37%)
  starting transfers between devices  33.7 us (13%)
  local copies, waits for them, and re-layouts  22.5 us (9%)
    pallas_call x2, Pallas kernels, kernel_products(): call(table_high, table_low, block, plane_both, lanes)  48 us
    all_to_all x3, waiting for transfers between devices, to_columns(): return lax.all_to_all(sent, 'rows', split_axis=0, concat_axis=0, tiled=True)  38.2 us
    ppermute x1, waiting for transfers between devices, aligned(): above = lax.ppermute(tail, 'rows', [(i, i + 1) for i in range(count - 1)])  30.7 us
    unnamed x36, local copies, waits for them, and re-layouts  20.3 us
    pallas_call x3, Pallas kernels, kernel_bins(): pl.pallas_call(bins_kernel, grid=(tiles,), out_shape=jax.ShapeDtypeStruct...  19.9 us
    ppermute x1, waiting for transfers between devices, per_device(): other = lax.ppermute(mine, 'group', [(0, 1), (1, 0)])  18.6 us
    all_to_all x3, starting transfers between devices, to_columns(): return lax.all_to_all(sent, 'rows', split_axis=0, concat_axis=0, tiled=True)  16.4 us
    all_to_all x2, starting transfers between devices, per_device(): lax.all_to_all(block, 'rows', split_axis=0, concat_axis=0, tiled=True)  11.8 us
  transfers between devices with their start and end apart: 8, of which 6 were waited for; matrix products, arithmetic and copies ran while one was open for 2% of the time, Pallas kernels for 30%

profile of v1, /device:TPU:15, one launch (start us, length us, event | category | flops | bytes accessed | tf_op | source)
XLA Modules:
  0.0 249.7 jit_solution(4952878609850454826)
XLA Ops:
  0.6 0.0 copy-start
  0.6 0.0 copy-start.4
  0.7 0.0 copy-start.5
  0.7 1.4 copy-done
  2.0 0.1 dynamic-slice_bitcast_fusion.rows
  2.1 0.0 copy-done.4
  2.1 0.2 copy-done.5
  2.3 0.0 copy-start.16
  2.3 6.5 %shard_map.150 = f32[48,32,128]{2,1,0:T(8,128)} custom-call(f32[1,6144]{1,0:T(1,128)S(1)} %broadcast_in_dim.19.keeper, f32[1,32,6144]{2,1,0:T(8,128)S(1)} %dynamic-slice_bitcast_fusion.rows, bf16[512,512]{1,0:T(8,128)(2,1)S(1)} %copy-done.4, bf16[512,512]{1,0:T(8,128)(2,1)S(1)} %copy-done.5), custom_call_target="tpu_custom_call" | custom-call | flops 603979776 | bytes 1572864 | tf_op jit(solution)/shard_map/pallas_call | solution.py:275
  8.8 6.6 %all-to-all-start.1 = ((f32[16,3,32,128]{3,2,1,0:T(8,128)}), f32[16,3,32,128]{3,2,1,0:T(8,128)S(1)}, u32[]{:S(2)}, u32[]{:S(2)}) async-start(f32[16,3,32,128]{3,2,1,0:T(8,128)} %bitcast.4), calls=%async_computation.1 | async-start | bytes 1572864 | tf_op jit(solution)/shard_map/all_to_all | solution.py:337
  15.3 0.0 copy-done.16
  15.3 0.1 select_bitcast_fusion
  15.5 0.0 copy-start.1
  15.5 1.9 copy-done.1
  17.3 6.7 %shard_map.153 = f32[48,64,128]{2,1,0:T(8,128)} custom-call(f32[1,6144]{1,0:T(1,128)S(1)} %bitcast.16, f32[2,64,6144]{2,1,0:T(8,128)S(1)} %copy-done.1, bf16[512,512]{1,0:T(8,128)(2,1)S(1)} %copy-done.4, bf16[512,512]{1,0:T(8,128)(2,1)S(1)} %copy-done.5), custom_call_target="tpu_custom_call" | custom-call | flops 1207959552 | bytes 3145728 | tf_op jit(solution)/shard_map/pallas_call | solution.py:275
  24.1 10.5 %all-to-all-done.1 = f32[16,3,32,128]{3,2,1,0:T(8,128)S(1)} async-done(((f32[16,3,32,128]{3,2,1,0:T(8,128)}), f32[16,3,32,128]{3,2,1,0:T(8,128)S(1)}, u32[]{:S(2)}, u32[]{:S(2)}) %all-to-all-start.1) | async-done | bytes 786464 | tf_op jit(solution)/shard_map/all_to_all | solution.py:337
  34.6 0.0 copy-start.15
  34.6 0.9 copy-done.15
  35.5 5.0 %all-to-all-start.3 = ((f32[16,3,64,128]{3,2,1,0:T(8,128)}), f32[16,3,64,128]{3,2,1,0:T(8,128)}, u32[]{:S(2)}, u32[]{:S(2)}) async-start(f32[16,3,64,128]{3,2,1,0:T(8,128)} %bitcast.6), calls=%async_computation.3 | async-start | bytes 3145728 | tf_op jit(solution)/shard_map/all_to_all | solution.py:337
  40.4 0.0 copy-start.2
  40.5 1.9 copy-done.2
  42.3 6.7 %shard_map.149 = f32[48,64,128]{2,1,0:T(8,128)} custom-call(f32[1,6144]{1,0:T(1,128)S(1)} %bitcast.17, f32[2,64,6144]{2,1,0:T(8,128)S(1)} %copy-done.2, bf16[512,512]{1,0:T(8,128)(2,1)S(1)} %copy-done.4, bf16[512,512]{1,0:T(8,128)(2,1)S(1)} %copy-done.5), custom_call_target="tpu_custom_call" | custom-call | flops 1207959552 | bytes 3145728 | tf_op jit(solution)/shard_map/pallas_call | solution.py:275
  49.1 27.7 %all-to-all-done.3.block = f32[16,3,64,128]{3,2,1,0:T(8,128)} async-done(((f32[16,3,64,128]{3,2,1,0:T(8,128)}), f32[16,3,64,128]{3,2,1,0:T(8,128)}, u32[]{:S(2)}, u32[]{:S(2)}) %all-to-all-start.3) | async-done | bytes 1572896 | tf_op jit(solution)/shard_map/all_to_all | solution.py:337
  76.7 4.9 %all-to-all-start = ((f32[16,3,64,128]{3,2,1,0:T(8,128)}), f32[16,3,64,128]{3,2,1,0:T(8,128)S(1)}, u32[]{:S(2)}, u32[]{:S(2)}) async-start(f32[16,3,64,128]{3,2,1,0:T(8,128)} %bitcast.2), calls=%async_computation | async-start | bytes 3145728 | tf_op jit(solution)/shard_map/all_to_all | solution.py:337
  81.6 0.3 collective-permute-start
  81.9 0.1 broadcast_and_fusion
  82.0 0.1 reshape.153.packed
  82.1 18.6 %collective-permute-done = f32[16,3,32,128]{3,2,1,0:T(8,128)} collective-permute-done((f32[16,3,32,128]{3,2,1,0:T(8,128)}, f32[16,3,32,128]{3,2,1,0:T(8,128)}, u32[]{:S(2)}, u32[]{:S(2)}) %collective-permute-start) | collective-permute-done | bytes 786464 | tf_op jit(solution)/shard_map/ppermute | solution.py:345
  100.7 0.0 copy-start.12
  100.7 1.7 broadcast_select_fusion.1
  102.5 0.1 pad_maximum_fusion.block
  102.6 0.8 copy-done.12
  103.4 10.3 %shard_map.151.plane_both = f32[2048,384]{1,0:T(8,128)S(1)} custom-call(bf16[2048,1024]{1,0:T(8,128)(2,1)S(1)} %copy-done.12, bf16[2048,1024]{1,0:T(8,128)(2,1)} %constant.54.clone.table_low, f32[16,3,64,128]{3,2,1,0:T(8,128)S(1)} %pad_maximum_fusion.block), custom_call_target="tpu_custom_call" | custom-call | flops 4831838208 | bytes 8388608 | tf_op jit(solution)/shard_map/pallas_call | solution.py:217
  113.7 24.2 %shard_map.154 = f32[16,3,64,128]{3,2,1,0:T(8,128)S(1)} custom-call(bf16[2048,1024]{1,0:T(8,128)(2,1)} %constant.53.clone.table_high, bf16[2048,1024]{1,0:T(8,128)(2,1)} %constant.54.clone.table_low, f32[16,3,64,128]{3,2,1,0:T(8,128)} %all-to-all-done.3.block, f32[2048,384]{1,0:T(8,128)S(1)} %shard_map.151.plane_both, f32[1,384]{1,0:T(1,128)S(1)} %reshape.153.packed), custom_call_target="tpu_custom_call" | custom-call | flops 9663676416 | bytes 8388608 | tf_op jit(solution)/shard_map/pallas_call | solution.py:241
  137.9 0.0 copy-start.9
  137.9 1.2 copy-done.9
  139.1 0.0 copy-start.13
  139.1 1.7 copy-done.13
  140.7 0.0 all-to-all-done.block
  140.8 0.0 copy-start.6
  140.8 1.1 copy-done.6
  141.9 6.8 %all-to-all-start.4 = ((f32[16,3,64,128]{3,2,1,0:T(8,128)}), f32[16,3,64,128]{3,2,1,0:T(8,128)S(1)}, u32[]{:S(2)}, u32[]{:S(2)}) async-start(f32[16,3,64,128]{3,2,1,0:T(8,128)} %copy-done.9), calls=%async_computation.4 | async-start | bytes 3145728 | tf_op jit(solution)/shard_map/all_to_all | solution.py:357
  148.7 0.0 copy-start.7
  148.7 1.4 copy-done.7
  150.2 0.0 copy-start.14
  150.2 1.9 copy-done.14
  152.0 23.8 %shard_map.152 = f32[16,3,64,128]{3,2,1,0:T(8,128)S(1)} custom-call(bf16[2048,1024]{1,0:T(8,128)(2,1)} %constant.53.clone.table_high, bf16[2048,1024]{1,0:T(8,128)(2,1)} %constant.54.clone.table_low, f32[16,3,64,128]{3,2,1,0:T(8,128)S(1)} %copy-done.7, f32[2048,384]{1,0:T(8,128)S(1)} %copy-done.14, f32[1,384]{1,0:T(1,128)S(1)} %reshape.153.packed), custom_call_target="tpu_custom_call" | custom-call | flops 9663676416 | bytes 8388608 | tf_op jit(solution)/shard_map/pallas_call | solution.py:241
  175.8 0.0 copy-start.8
  175.8 1.1 copy-done.8
  177.0 7.9 %all-to-all-done.4 = f32[16,3,64,128]{3,2,1,0:T(8,128)S(1)} async-done(((f32[16,3,64,128]{3,2,1,0:T(8,128)}), f32[16,3,64,128]{3,2,1,0:T(8,128)S(1)}, u32[]{:S(2)}, u32[]{:S(2)}) %all-to-all-start.4) | async-done | bytes 1572896 | tf_op jit(solution)/shard_map/all_to_all | solution.py:357
  184.9 4.9 %all-to-all-start.2 = ((f32[16,3,64,128]{3,2,1,0:T(8,128)}), f32[16,3,64,128]{3,2,1,0:T(8,128)}, u32[]{:S(2)}, u32[]{:S(2)}) async-start(f32[16,3,64,128]{3,2,1,0:T(8,128)} %copy-done.8), calls=%async_computation.2 | async-start | bytes 3145728 | tf_op jit(solution)/shard_map/all_to_all | solution.py:357
  189.8 2.1 fusion.3
  191.9 3.3 %collective-permute-start.1 = (f32[2,8,6144]{2,1,0:T(8,128)}, f32[2,8,6144]{2,1,0:T(8,128)S(1)}, u32[]{:S(2)}, u32[]{:S(2)}) collective-permute-start(f32[2,8,6144]{2,1,0:T(8,128)} %get-tuple-element.3), channel_id=1, source_target_pairs={{0,1},{1,2},{2,3},{3,4},{4,5},{5,6},{6,7},{7,8},{8,9},{9,10},{10,1... | collective-permute-start | bytes 1179656 | tf_op jit(solution)/shard_map/ppermute | solution.py:73
  195.2 1.9 collective-permute-start.2
  197.2 0.8 copy.16.shifts
  197.9 30.7 %collective-permute-done.1.above = f32[2,8,6144]{2,1,0:T(8,128)S(1)} collective-permute-done((f32[2,8,6144]{2,1,0:T(8,128)}, f32[2,8,6144]{2,1,0:T(8,128)S(1)}, u32[]{:S(2)}, u32[]{:S(2)}) %collective-permute-start.1) | collective-permute-done | bytes 393248 | tf_op jit(solution)/shard_map/ppermute | solution.py:73
  228.7 1.6 collective-permute-done.2.below
  230.2 0.0 copy-start.3
  230.2 1.9 copy-done.3
  232.1 4.1 %shard_map.156 = f32[2,64,6144]{2,1,0:T(8,128)} custom-call(s32[2,12,2]{2,1,0:T(8,128)S(1)} %copy.16.shifts, f32[2,64,6144]{2,1,0:T(8,128)S(1)} %copy-done.3, f32[2,8,6144]{2,1,0:T(8,128)S(1)} %collective-permute-done.1.above, f32[2,8,6144]{2,1,0:T(8,128)} %collective-permute-done.2.below), custom_call_target="tpu_custom_call" | custom-call | flops 15728640 | bytes 6291456 | tf_op jit(solution)/shard_map/pallas_call | solution.py:77
  236.3 0.0 all-to-all-done.2
  236.3 1.0 copy-done.10
  237.3 1.0 copy-done.11
  238.4 11.3 %shard_map.155 = f32[2,64,6144]{2,1,0:T(8,128)} custom-call(f32[48,64,128]{2,1,0:T(8,128)} %bitcast.5.refs_0_, f32[48,64,128]{2,1,0:T(8,128)S(1)} %bitcast.15, bf16[512,512]{1,0:T(8,128)(2,1)S(1)} %copy-done.10, bf16[512,512]{1,0:T(8,128)(2,1)S(1)} %copy-done.11), custom_call_target="tpu_custom_call" | custom-call | tf_op jit(solution)/shard_map/pallas_call | solution.py:299
  (8 shorter events, 0.1 us)
Async XLA Ops:
  0.6 1.4 copy-start
  0.6 1.5 copy-start.4
  0.7 1.6 copy-start.5
  2.3 13.0 %copy-start.16 = (s32[12,2]{0,1:T(2,128)S(1)}, s32[12,2]{0,1:T(2,128)}, u32[]{:S(2)}) copy-start(s32[12,2]{0,1:T(2,128)} %param.16) | copy-start | bytes 292
  8.8 25.8 %all-to-all-start.1 = ((f32[16,3,32,128]{3,2,1,0:T(8,128)}), f32[16,3,32,128]{3,2,1,0:T(8,128)S(1)}, u32[]{:S(2)}, u32[]{:S(2)}) async-start(f32[16,3,32,128]{3,2,1,0:T(8,128)} %bitcast.4), calls=%async_computation.1 | async-start | bytes 1572864 | tf_op jit(solution)/shard_map/all_to_all | solution.py:337
  15.5 1.9 copy-start.1
  34.6 0.9 copy-start.15
  35.5 41.2 %all-to-all-start.3 = ((f32[16,3,64,128]{3,2,1,0:T(8,128)}), f32[16,3,64,128]{3,2,1,0:T(8,128)}, u32[]{:S(2)}, u32[]{:S(2)}) async-start(f32[16,3,64,128]{3,2,1,0:T(8,128)} %bitcast.6), calls=%async_computation.3 | async-start | bytes 3145728 | tf_op jit(solution)/shard_map/all_to_all | solution.py:337
  40.4 1.9 copy-start.2
  76.7 64.0 %all-to-all-start = ((f32[16,3,64,128]{3,2,1,0:T(8,128)}), f32[16,3,64,128]{3,2,1,0:T(8,128)S(1)}, u32[]{:S(2)}, u32[]{:S(2)}) async-start(f32[16,3,64,128]{3,2,1,0:T(8,128)} %bitcast.2), calls=%async_computation | async-start | bytes 3145728 | tf_op jit(solution)/shard_map/all_to_all | solution.py:337
  81.6 19.1 %collective-permute-start = (f32[16,3,32,128]{3,2,1,0:T(8,128)}, f32[16,3,32,128]{3,2,1,0:T(8,128)}, u32[]{:S(2)}, u32[]{:S(2)}) collective-permute-start(f32[16,3,32,128]{3,2,1,0:T(8,128)} %copy-done.15), channel_id=1, source_target_pairs={{0,16},{16,0},{1,17},{17,1},{2,18},{18,2},{3,19},{19,3},{4,20},{20... | collective-permute-start | bytes 2359304 | tf_op jit(solution)/shard_map/ppermute | solution.py:345
  100.7 2.7 %copy-start.12 = (bf16[2048,1024]{1,0:T(8,128)(2,1)S(1)}, bf16[2048,1024]{1,0:T(8,128)(2,1)}, u32[]{:S(2)}) copy-start(bf16[2048,1024]{1,0:T(8,128)(2,1)} %constant.53.clone.table_high) | copy-start | bytes 12582916
  137.9 1.2 copy-start.9
  139.1 1.7 copy-start.13
  140.8 1.1 copy-start.6
  141.9 43.0 %all-to-all-start.4 = ((f32[16,3,64,128]{3,2,1,0:T(8,128)}), f32[16,3,64,128]{3,2,1,0:T(8,128)S(1)}, u32[]{:S(2)}, u32[]{:S(2)}) async-start(f32[16,3,64,128]{3,2,1,0:T(8,128)} %copy-done.9), calls=%async_computation.4 | async-start | bytes 3145728 | tf_op jit(solution)/shard_map/all_to_all | solution.py:357
  148.7 1.4 copy-start.7
  150.2 1.9 copy-start.14
  175.8 1.1 copy-start.8
  184.9 51.3 %all-to-all-start.2 = ((f32[16,3,64,128]{3,2,1,0:T(8,128)}), f32[16,3,64,128]{3,2,1,0:T(8,128)}, u32[]{:S(2)}, u32[]{:S(2)}) async-start(f32[16,3,64,128]{3,2,1,0:T(8,128)} %copy-done.8), calls=%async_computation.2 | async-start | bytes 3145728 | tf_op jit(solution)/shard_map/all_to_all | solution.py:357
  191.9 36.8 %collective-permute-start.1 = (f32[2,8,6144]{2,1,0:T(8,128)}, f32[2,8,6144]{2,1,0:T(8,128)S(1)}, u32[]{:S(2)}, u32[]{:S(2)}) collective-permute-start(f32[2,8,6144]{2,1,0:T(8,128)} %get-tuple-element.3), channel_id=1, source_target_pairs={{0,1},{1,2},{2,3},{3,4},{4,5},{5,6},{6,7},{7,8},{8,9},{9,10},{10,1... | collective-permute-start | bytes 1179656 | tf_op jit(solution)/shard_map/ppermute | solution.py:73
  195.2 35.0 %collective-permute-start.2 = (f32[2,8,6144]{2,1,0:T(8,128)}, f32[2,8,6144]{2,1,0:T(8,128)}, u32[]{:S(2)}, u32[]{:S(2)}) collective-permute-start(f32[2,8,6144]{2,1,0:T(8,128)} %get-tuple-element.2), channel_id=1, source_target_pairs={{1,0},{2,1},{3,2},{4,3},{5,4},{6,5},{7,6},{8,7},{9,8},{10,9},{11,1... | collective-permute-start | bytes 1179656 | tf_op jit(solution)/shard_map/ppermute | solution.py:74
  230.2 1.9 copy-start.3
  236.3 1.0 copy-start.10
  237.3 1.0 copy-start.11

commit v2 on v1

--- a/solution.py
+++ b/solution.py
@@ -202,43 +202,45 @@
                 ]
 
 
-def kernel_products(plane_columns, received, packed):
-    count, local, height, width = plane_columns.shape
-    breadth = local * width
-    table = column_table().reshape(2 * F1, F1)
-    table_high = table.astype(jnp.bfloat16)
-    table_low = (table - table_high.astype(np.float64)).astype(jnp.bfloat16)
-    lanes = jnp.stack([packed, packed], axis=1).reshape(1, breadth).astype(jnp.float32)
-    flops = 12 * F1 * F1 * breadth
+def column_parts():
+    return split_table(column_table().reshape(2 * F1, F1))
+
+
+def kernel_plane(plane_columns):
+    breadth = plane_columns.shape[1] * plane_columns.shape[3]
     space = pl.BlockSpec(memory_space=pltpu.VMEM)
-    params = pltpu.CompilerParams(vmem_limit_bytes=44 * 2**20)
-    halves_shape = (2 * F1, breadth)
-    scratch = [pltpu.VMEM((F1, breadth), jnp.bfloat16)] * 2
-    plane_both = pl.pallas_call(
+    return pl.pallas_call(
         forward_halves,
-        out_shape=jax.ShapeDtypeStruct(halves_shape, jnp.float32),
+        out_shape=jax.ShapeDtypeStruct((2 * F1, breadth), jnp.float32),
         in_specs=[space] * 3,
         out_specs=space,
-        scratch_shapes=scratch,
-        compiler_params=params,
+        scratch_shapes=[pltpu.VMEM((F1, breadth), jnp.bfloat16)] * 2,
+        compiler_params=pltpu.CompilerParams(vmem_limit_bytes=44 * 2**20),
         cost_estimate=pl.CostEstimate(
-            flops=flops, bytes_accessed=8 * F1 * F1, transcendentals=0
+            flops=12 * F1 * F1 * breadth, bytes_accessed=8 * F1 * F1, transcendentals=0
         ),
-    )(table_high, table_low, plane_columns)
+    )(*column_parts(), plane_columns)
+
+
+def kernel_products(plane_both, received, packed):
+    breadth = plane_both.shape[1]
+    lanes = jnp.stack([packed, packed], axis=1).reshape(1, breadth).astype(jnp.float32)
+    space = pl.BlockSpec(memory_space=pltpu.VMEM)
+    halves_shape = (2 * F1, breadth)
     call = pl.pallas_call(
         product_kernel,
-        out_shape=jax.ShapeDtypeStruct(plane_columns.shape, jnp.float32),
+        out_shape=jax.ShapeDtypeStruct(received[0].shape, jnp.float32),
         in_specs=[space] * 5,
         out_specs=space,
         scratch_shapes=[pltpu.VMEM(halves_shape, jnp.float32)]
-        + scratch
+        + [pltpu.VMEM((F1, breadth), jnp.bfloat16)] * 2
         + [pltpu.VMEM(halves_shape, jnp.bfloat16)] * 2,
-        compiler_params=params,
+        compiler_params=pltpu.CompilerParams(vmem_limit_bytes=44 * 2**20),
         cost_estimate=pl.CostEstimate(
-            flops=2 * flops, bytes_accessed=8 * F1 * F1, transcendentals=0
+            flops=24 * F1 * F1 * breadth, bytes_accessed=8 * F1 * F1, transcendentals=0
         ),
     )
-    return [call(table_high, table_low, block, plane_both, lanes) for block in received]
+    return [call(*column_parts(), block, plane_both, lanes) for block in received]
 
 
 def product_of(values, table_high, table_low):
@@ -247,20 +249,40 @@
     def dot(a, b):
         return jnp.dot(a, b, preferred_element_type=jnp.float32)
 
-    return dot(high, table_high) + (dot(low, table_high) + dot(high, table_low))
+    count = values.shape[0]
+    both = dot(jnp.concatenate([high, low], axis=0), table_high)
+    return both[:count] + (both[count:] + dot(high, table_low))
 
 
 def bins_kernel(keeper, rows, table_high, table_low, out):
-    bins = product_of(rows[...] * keeper[...], table_high[...], table_low[...])
-    for group in range(out.shape[0]):
-        out[group] = bins[:, group * LANES : (group + 1) * LANES]
+    height, breadth = rows.shape
+    groups = TF2 // LANES
+    values = rows[...] * keeper[...]
+    tiles = [values[:, start : start + TF2] for start in range(0, breadth, TF2)]
+    bins = product_of(jnp.concatenate(tiles, axis=0), table_high[...], table_low[...])
+    for tile in range(len(tiles)):
+        for group in range(groups):
+            out[tile * groups + group] = bins[
+                tile * height : (tile + 1) * height, group * LANES : (group + 1) * LANES
+            ]
 
 
 def rows_kernel(*refs):
     blocks, (table_high, table_low, out) = refs[:-3], refs[-3:]
-    for spectrum, block in enumerate(blocks):
-        bins = jnp.concatenate([block[group] for group in range(block.shape[0])], axis=1)
-        out[spectrum] = product_of(bins, table_high[...], table_low[...])
+    granules, height = blocks[0].shape[:2]
+    groups = TF2 // LANES
+    places = [(s, t) for s in range(len(blocks)) for t in range(granules // groups)]
+    parts = [
+        jnp.concatenate([blocks[s][t * groups + group] for group in range(groups)], axis=1)
+        for s, t in places
+    ]
+    rows = product_of(jnp.concatenate(parts, axis=0), table_high[...], table_low[...])
+    for place, (s, t) in enumerate(places):
+        out[s, :, t * TF2 : (t + 1) * TF2] = rows[place * height : (place + 1) * height]
+
+
+def tiles_at_once(tiles):
+    return 3 if tiles % 3 == 0 else 2 if tiles % 2 == 0 else 1
 
 
 def split_table(table):
@@ -271,18 +293,19 @@
 def kernel_bins(spectra, index, keeper, table):
     height, breadth = spectra.shape[1:]
     tiles, groups = breadth // TF2, TF2 // LANES
+    step = tiles_at_once(tiles)
     fixed = pl.BlockSpec((TF2, TF2), lambda b: (0, 0))
     return pl.pallas_call(
         bins_kernel,
-        grid=(tiles,),
+        grid=(tiles // step,),
         out_shape=jax.ShapeDtypeStruct((tiles * groups, height, LANES), jnp.float32),
         in_specs=[
-            pl.BlockSpec((1, TF2), lambda b: (0, b)),
-            pl.BlockSpec((None, height, TF2), lambda b: (index, 0, b)),
+            pl.BlockSpec((1, step * TF2), lambda b: (0, b)),
+            pl.BlockSpec((None, height, step * TF2), lambda b: (index, 0, b)),
             fixed,
             fixed,
         ],
-        out_specs=pl.BlockSpec((groups, height, LANES), lambda b: (b, 0, 0)),
+        out_specs=pl.BlockSpec((step * groups, height, LANES), lambda b: (b, 0, 0)),
         compiler_params=pltpu.CompilerParams(vmem_limit_bytes=24 * 2**20),
         cost_estimate=pl.CostEstimate(
             flops=6 * height * breadth * TF2, bytes_accessed=8 * height * breadth, transcendentals=0
@@ -295,14 +318,15 @@
     groups = TF2 // LANES
     tiles = granules // groups
     number = len(blocks)
+    step = tiles_at_once(tiles)
     fixed = pl.BlockSpec((TF2, TF2), lambda b: (0, 0))
     return pl.pallas_call(
         rows_kernel,
-        grid=(tiles,),
+        grid=(tiles // step,),
         out_shape=jax.ShapeDtypeStruct((number, height, tiles * TF2), jnp.float32),
-        in_specs=[pl.BlockSpec((groups, height, LANES), lambda b: (b, 0, 0))] * number
+        in_specs=[pl.BlockSpec((step * groups, height, LANES), lambda b: (b, 0, 0))] * number
         + [fixed, fixed],
-        out_specs=pl.BlockSpec((number, height, TF2), lambda b: (0, 0, b)),
+        out_specs=pl.BlockSpec((number, height, step * TF2), lambda b: (0, 0, b)),
         compiler_params=pltpu.CompilerParams(vmem_limit_bytes=24 * 2**20),
     )(*blocks, *split_table(table))
 
@@ -325,7 +349,7 @@
     share = height // cohorts
     whole_tiles = width == LANES and share % 16 == 0
 
-    def to_columns(rows, index, kept):
+    def to_columns(rows, index, kept, after=None):
         held = rows.shape[1]
         if whole_tiles:
             bins = kernel_bins(rows, index, kept, forward.reshape(TF2, TF2))
@@ -334,6 +358,8 @@
             table = forward.astype(np.float32)
             bins = jnp.einsum("rbn,njl->bjrl", blocks, table, precision=full)
         sent = bins.reshape(count, local, held, width)
+        if after is not None:
+            sent, _ = lax.optimization_barrier((sent, after))
         return lax.all_to_all(sent, "rows", split_axis=0, concat_axis=0, tiled=True)
 
     granule = lax.axis_index("rows") * local + jnp.arange(local, dtype=jnp.int32)
@@ -347,10 +373,11 @@
         plane_columns = jnp.concatenate(ordered, axis=2)
     else:
         plane_columns = lax.all_gather(mine, "group", axis=2, tiled=True)
-    received = [to_columns(spectra, s, keeper) for s in range(number)]
+    plane_both = kernel_plane(plane_columns) if whole_tiles else None
+    received = [to_columns(spectra, s, keeper, plane_both if s else None) for s in range(number)]
     aligned_spectra = aligned(spectra, tile_shifts)
     if whole_tiles:
-        products = kernel_products(plane_columns, received, packed)
+        products = kernel_products(plane_both, received, packed)
     else:
         products = plain_products(plane_columns, received, packed)
     returned = [

time: 251 us -> 215 us (0.86)
  Pallas kernels: 93.7 us -> 76.4 us
  waiting for transfers between devices: 97.1 us -> 80 us
    pallas_call x7, Pallas kernels: 89.5 us -> 72.3 us  [the longest x2 48 us: kernel_products(): call(*column_parts(), block, plane_both, lanes)]
    all_to_all x3, waiting for transfers between devices: 38.2 us -> 26 us  [to_columns(): return lax.all_to_all(sent, 'rows', split_axis=0, concat_axis=0, tiled=True)]
    ppermute x1, waiting for transfers between devices: 18.6 us -> 13.7 us  [per_device(): other = lax.ppermute(mine, 'group', [(0, 1), (1, 0)])]
  transfers between devices with their start and end apart: 8 -> 8, of which waited for: 6 -> 7; matrix products, arithmetic and copies ran while one was open for 2% -> 2% of each run, Pallas kernels for 30% -> 32%
where the time goes in v2:
time: 215 us; the launch traced here: 214 us
  waiting for transfers between devices  80 us (37%)
  Pallas kernels  76.4 us (36%)
  starting transfers between devices  31.7 us (15%)
  local copies, waits for them, and re-layouts  23.4 us (11%)
    pallas_call x2, Pallas kernels, kernel_products(): call(*column_parts(), block, plane_both, lanes)  48 us
    ppermute x1, waiting for transfers between devices, aligned(): above = lax.ppermute(tail, 'rows', [(i, i + 1) for i in range(count - 1)])  30.7 us
    all_to_all x3, waiting for transfers between devices, to_columns(): return lax.all_to_all(sent, 'rows', split_axis=0, concat_axis=0, tiled=True)  26 us
    unnamed x36, local copies, waits for them, and re-layouts  21.2 us
    all_to_all x3, starting transfers between devices, to_columns(): return lax.all_to_all(sent, 'rows', split_axis=0, concat_axis=0, tiled=True)  16.4 us
    ppermute x1, waiting for transfers between devices, per_device(): other = lax.ppermute(mine, 'group', [(0, 1), (1, 0)])  13.7 us
    pallas_call x1, Pallas kernels, kernel_plane(): pl.pallas_call(forward_halves, out_shape=jax.ShapeDtypeStruct((2 * F1, br...  10.3 us
    all_to_all x2, starting transfers between devices, per_device(): lax.all_to_all(block, 'rows', split_axis=0, concat_axis=0, tiled=True)  9.82 us
  transfers between devices with their start and end apart: 8, of which 7 were waited for; matrix products, arithmetic and copies ran while one was open for 2% of the time, Pallas kernels for 32%

profile of v2, /device:TPU:15, one launch (start us, length us, event | category | flops | bytes accessed | tf_op | source)
XLA Modules:
  0.0 214.1 jit_solution(595569011436196446)
XLA Ops:
  0.6 0.0 copy-start
  0.6 0.0 copy-start.4
  0.7 0.0 copy-start.5
  0.7 1.4 copy-done
  2.0 0.1 dynamic-slice_bitcast_fusion.rows
  2.1 0.0 copy-done.4
  2.1 0.2 copy-done.5
  2.3 0.0 copy-start.16
  2.3 2.5 %shard_map.186 = f32[48,32,128]{2,1,0:T(8,128)} custom-call(f32[1,6144]{1,0:T(1,128)S(1)} %broadcast_in_dim.19.keeper, f32[1,32,6144]{2,1,0:T(8,128)S(1)} %dynamic-slice_bitcast_fusion.rows, bf16[512,512]{1,0:T(8,128)(2,1)S(1)} %copy-done.4, bf16[512,512]{1,0:T(8,128)(2,1)S(1)} %copy-done.5), custom_call_target="tpu_custom_call" | custom-call | flops 603979776 | bytes 1572864 | tf_op jit(solution)/shard_map/pallas_call | solution.py:298
  4.8 6.6 %all-to-all-start.1 = ((f32[16,3,32,128]{3,2,1,0:T(8,128)}), f32[16,3,32,128]{3,2,1,0:T(8,128)S(1)}, u32[]{:S(2)}, u32[]{:S(2)}) async-start(f32[16,3,32,128]{3,2,1,0:T(8,128)} %bitcast.4), calls=%async_computation.1 | async-start | bytes 1572864 | tf_op jit(solution)/shard_map/all_to_all | solution.py:363
  11.3 0.0 copy-done.16
  11.3 0.1 select_bitcast_fusion
  11.4 0.0 copy-start.1
  11.5 1.9 copy-done.1
  13.3 3.0 %shard_map.185 = f32[48,64,128]{2,1,0:T(8,128)} custom-call(f32[1,6144]{1,0:T(1,128)S(1)} %bitcast.16, f32[2,64,6144]{2,1,0:T(8,128)S(1)} %copy-done.1, bf16[512,512]{1,0:T(8,128)(2,1)S(1)} %copy-done.4, bf16[512,512]{1,0:T(8,128)(2,1)S(1)} %copy-done.5), custom_call_target="tpu_custom_call" | custom-call | flops 1207959552 | bytes 3145728 | tf_op jit(solution)/shard_map/pallas_call | solution.py:298
  16.3 14.2 %all-to-all-done.1 = f32[16,3,32,128]{3,2,1,0:T(8,128)S(1)} async-done(((f32[16,3,32,128]{3,2,1,0:T(8,128)}), f32[16,3,32,128]{3,2,1,0:T(8,128)S(1)}, u32[]{:S(2)}, u32[]{:S(2)}) %all-to-all-start.1) | async-done | bytes 786464 | tf_op jit(solution)/shard_map/all_to_all | solution.py:363
  30.6 5.0 %all-to-all-start = ((f32[16,3,64,128]{3,2,1,0:T(8,128)}), f32[16,3,64,128]{3,2,1,0:T(8,128)}, u32[]{:S(2)}, u32[]{:S(2)}) async-start(f32[16,3,64,128]{3,2,1,0:T(8,128)} %bitcast.2), calls=%async_computation | async-start | bytes 3145728 | tf_op jit(solution)/shard_map/all_to_all | solution.py:363
  35.5 0.2 collective-permute-start
  35.8 0.0 copy-start.2
  35.8 1.9 copy-done.2
  37.6 3.0 %shard_map.189 = f32[48,64,128]{2,1,0:T(8,128)} custom-call(f32[1,6144]{1,0:T(1,128)S(1)} %bitcast.17, f32[2,64,6144]{2,1,0:T(8,128)S(1)} %copy-done.2, bf16[512,512]{1,0:T(8,128)(2,1)S(1)} %copy-done.4, bf16[512,512]{1,0:T(8,128)(2,1)S(1)} %copy-done.5), custom_call_target="tpu_custom_call" | custom-call | flops 1207959552 | bytes 3145728 | tf_op jit(solution)/shard_map/pallas_call | solution.py:298
  40.7 13.7 %collective-permute-done = f32[16,3,32,128]{3,2,1,0:T(8,128)} collective-permute-done((f32[16,3,32,128]{3,2,1,0:T(8,128)S(1)}, f32[16,3,32,128]{3,2,1,0:T(8,128)}, u32[]{:S(2)}, u32[]{:S(2)}) %collective-permute-start) | collective-permute-done | bytes 786464 | tf_op jit(solution)/shard_map/ppermute | solution.py:371
  54.4 0.0 copy-start.12
  54.4 1.5 broadcast_select_fusion.1
  55.9 0.1 pad_maximum_fusion.block
  56.0 0.8 copy-done.12
  56.8 10.3 %shard_map.187.plane_both = f32[2048,384]{1,0:T(8,128)S(1)} custom-call(bf16[2048,1024]{1,0:T(8,128)(2,1)S(1)} %copy-done.12, bf16[2048,1024]{1,0:T(8,128)(2,1)} %constant.54.clone.table_low, f32[16,3,64,128]{3,2,1,0:T(8,128)S(1)} %pad_maximum_fusion.block), custom_call_target="tpu_custom_call" | custom-call | flops 4831838208 | bytes 8388608 | tf_op jit(solution)/shard_map/pallas_call | solution.py:212
  67.1 0.0 copy-start.13
  67.1 1.7 copy-done.13
  68.8 3.0 %all-to-all-done.block = f32[16,3,64,128]{3,2,1,0:T(8,128)} async-done(((f32[16,3,64,128]{3,2,1,0:T(8,128)}), f32[16,3,64,128]{3,2,1,0:T(8,128)}, u32[]{:S(2)}, u32[]{:S(2)}) %all-to-all-start) | async-done | bytes 1572896 | tf_op jit(solution)/shard_map/all_to_all | solution.py:363
  71.8 4.9 %all-to-all-start.3 = ((f32[16,3,64,128]{3,2,1,0:T(8,128)}), f32[16,3,64,128]{3,2,1,0:T(8,128)S(1)}, u32[]{:S(2)}, u32[]{:S(2)}) async-start(f32[16,3,64,128]{3,2,1,0:T(8,128)} %bitcast.6), calls=%async_computation.3 | async-start | bytes 3145728 | tf_op jit(solution)/shard_map/all_to_all | solution.py:363
  76.7 0.1 broadcast_and_fusion
  76.8 0.1 reshape.153.packed
  76.9 0.0 copy-start.14
  76.9 1.9 copy-done.14
  78.8 24.2 %shard_map.188 = f32[16,3,64,128]{3,2,1,0:T(8,128)S(1)} custom-call(bf16[2048,1024]{1,0:T(8,128)(2,1)} %constant.53.clone.table_high, bf16[2048,1024]{1,0:T(8,128)(2,1)} %constant.54.clone.table_low, f32[16,3,64,128]{3,2,1,0:T(8,128)} %all-to-all-done.block, f32[2048,384]{1,0:T(8,128)S(1)} %copy-done.14, f32[1,384]{1,0:T(1,128)S(1)} %reshape.153.packed), custom_call_target="tpu_custom_call" | custom-call | flops 9663676416 | bytes 8388608 | tf_op jit(solution)/shard_map/pallas_call | solution.py:243
  103.0 0.0 copy-start.9
  103.0 1.1 copy-done.9
  104.1 8.7 %all-to-all-done.3.block = f32[16,3,64,128]{3,2,1,0:T(8,128)S(1)} async-done(((f32[16,3,64,128]{3,2,1,0:T(8,128)}), f32[16,3,64,128]{3,2,1,0:T(8,128)S(1)}, u32[]{:S(2)}, u32[]{:S(2)}) %all-to-all-start.3) | async-done | bytes 1572896 | tf_op jit(solution)/shard_map/all_to_all | solution.py:363
  112.9 0.0 copy-start.7
  112.9 1.2 copy-done.7
  114.1 4.9 %all-to-all-start.2 = ((f32[16,3,64,128]{3,2,1,0:T(8,128)}), f32[16,3,64,128]{3,2,1,0:T(8,128)S(1)}, u32[]{:S(2)}, u32[]{:S(2)}) async-start(f32[16,3,64,128]{3,2,1,0:T(8,128)} %copy-done.9), calls=%async_computation.2 | async-start | bytes 3145728 | tf_op jit(solution)/shard_map/all_to_all | solution.py:384
  119.0 0.0 copy-start.8
  119.0 1.4 copy-done.8
  120.4 0.0 copy-start.15
  120.4 1.9 copy-done.15
  122.3 23.8 %shard_map.190 = f32[16,3,64,128]{3,2,1,0:T(8,128)S(1)} custom-call(bf16[2048,1024]{1,0:T(8,128)(2,1)} %constant.53.clone.table_high, bf16[2048,1024]{1,0:T(8,128)(2,1)} %constant.54.clone.table_low, f32[16,3,64,128]{3,2,1,0:T(8,128)S(1)} %copy-done.8, f32[2048,384]{1,0:T(8,128)S(1)} %copy-done.15, f32[1,384]{1,0:T(1,128)S(1)} %reshape.153.packed), custom_call_target="tpu_custom_call" | custom-call | flops 9663676416 | bytes 8388608 | tf_op jit(solution)/shard_map/pallas_call | solution.py:243
  146.1 0.0 copy-start.6
  146.1 1.1 copy-done.6
  147.2 7.9 %all-to-all-done.2 = f32[16,3,64,128]{3,2,1,0:T(8,128)S(1)} async-done(((f32[16,3,64,128]{3,2,1,0:T(8,128)}), f32[16,3,64,128]{3,2,1,0:T(8,128)S(1)}, u32[]{:S(2)}, u32[]{:S(2)}) %all-to-all-start.2) | async-done | bytes 1572896 | tf_op jit(solution)/shard_map/all_to_all | solution.py:384
  155.2 4.9 %all-to-all-start.4 = ((f32[16,3,64,128]{3,2,1,0:T(8,128)}), f32[16,3,64,128]{3,2,1,0:T(8,128)}, u32[]{:S(2)}, u32[]{:S(2)}) async-start(f32[16,3,64,128]{3,2,1,0:T(8,128)} %copy-done.6), calls=%async_computation.4 | async-start | bytes 3145728 | tf_op jit(solution)/shard_map/all_to_all | solution.py:384
  160.1 2.0 fusion.3
  162.1 3.3 %collective-permute-start.1 = (f32[2,8,6144]{2,1,0:T(8,128)}, f32[2,8,6144]{2,1,0:T(8,128)S(1)}, u32[]{:S(2)}, u32[]{:S(2)}) collective-permute-start(f32[2,8,6144]{2,1,0:T(8,128)} %get-tuple-element.5), channel_id=1, source_target_pairs={{0,1},{1,2},{2,3},{3,4},{4,5},{5,6},{6,7},{7,8},{8,9},{9,10},{10,1... | collective-permute-start | bytes 1179656 | tf_op jit(solution)/shard_map/ppermute | solution.py:73
  165.5 1.9 collective-permute-start.2
  167.4 0.8 copy.20.shifts
  168.2 30.7 %collective-permute-done.1.above = f32[2,8,6144]{2,1,0:T(8,128)S(1)} collective-permute-done((f32[2,8,6144]{2,1,0:T(8,128)}, f32[2,8,6144]{2,1,0:T(8,128)S(1)}, u32[]{:S(2)}, u32[]{:S(2)}) %collective-permute-start.1) | collective-permute-done | bytes 393248 | tf_op jit(solution)/shard_map/ppermute | solution.py:73
  198.9 1.6 collective-permute-done.2.below
  200.5 0.0 copy-start.3
  200.5 1.9 copy-done.3
  202.4 4.1 %shard_map.192 = f32[2,64,6144]{2,1,0:T(8,128)} custom-call(s32[2,12,2]{2,1,0:T(8,128)S(1)} %copy.20.shifts, f32[2,64,6144]{2,1,0:T(8,128)S(1)} %copy-done.3, f32[2,8,6144]{2,1,0:T(8,128)S(1)} %collective-permute-done.1.above, f32[2,8,6144]{2,1,0:T(8,128)} %collective-permute-done.2.below), custom_call_target="tpu_custom_call" | custom-call | flops 15728640 | bytes 6291456 | tf_op jit(solution)/shard_map/pallas_call | solution.py:77
  206.5 0.0 all-to-all-done.4
  206.5 1.0 copy-done.10
  207.6 1.0 copy-done.11
  208.6 5.5 %shard_map.191 = f32[2,64,6144]{2,1,0:T(8,128)} custom-call(f32[48,64,128]{2,1,0:T(8,128)S(1)} %bitcast.15, f32[48,64,128]{2,1,0:T(8,128)} %bitcast.7.refs_1_, bf16[512,512]{1,0:T(8,128)(2,1)S(1)} %copy-done.10, bf16[512,512]{1,0:T(8,128)(2,1)S(1)} %copy-done.11), custom_call_target="tpu_custom_call" | custom-call | tf_op jit(solution)/shard_map/pallas_call | solution.py:323
  (8 shorter events, 0.1 us)
Async XLA Ops:
  0.6 1.4 copy-start
  0.6 1.5 copy-start.4
  0.7 1.6 copy-start.5
  2.3 9.0 %copy-start.16 = (s32[12,2]{0,1:T(2,128)S(1)}, s32[12,2]{0,1:T(2,128)}, u32[]{:S(2)}) copy-start(s32[12,2]{0,1:T(2,128)} %param.20) | copy-start | bytes 292
  4.8 25.8 %all-to-all-start.1 = ((f32[16,3,32,128]{3,2,1,0:T(8,128)}), f32[16,3,32,128]{3,2,1,0:T(8,128)S(1)}, u32[]{:S(2)}, u32[]{:S(2)}) async-start(f32[16,3,32,128]{3,2,1,0:T(8,128)} %bitcast.4), calls=%async_computation.1 | async-start | bytes 1572864 | tf_op jit(solution)/shard_map/all_to_all | solution.py:363
  11.4 1.9 copy-start.1
  30.6 41.2 %all-to-all-start = ((f32[16,3,64,128]{3,2,1,0:T(8,128)}), f32[16,3,64,128]{3,2,1,0:T(8,128)}, u32[]{:S(2)}, u32[]{:S(2)}) async-start(f32[16,3,64,128]{3,2,1,0:T(8,128)} %bitcast.2), calls=%async_computation | async-start | bytes 3145728 | tf_op jit(solution)/shard_map/all_to_all | solution.py:363
  35.5 18.9 %collective-permute-start = (f32[16,3,32,128]{3,2,1,0:T(8,128)S(1)}, f32[16,3,32,128]{3,2,1,0:T(8,128)}, u32[]{:S(2)}, u32[]{:S(2)}) collective-permute-start(f32[16,3,32,128]{3,2,1,0:T(8,128)S(1)} %all-to-all-done.1), channel_id=1, source_target_pairs={{0,16},{16,0},{1,17},{17,1},{2,18},{18,2},{3,19},{19,3},{4,20},{20... | collective-permute-start | bytes 2359304 | tf_op jit(solution)/shard_map/ppermute | solution.py:371
  35.8 1.9 copy-start.2
  54.4 2.4 %copy-start.12 = (bf16[2048,1024]{1,0:T(8,128)(2,1)S(1)}, bf16[2048,1024]{1,0:T(8,128)(2,1)}, u32[]{:S(2)}) copy-start(bf16[2048,1024]{1,0:T(8,128)(2,1)} %constant.53.clone.table_high) | copy-start | bytes 12582916
  67.1 1.7 copy-start.13
  71.8 41.1 %all-to-all-start.3 = ((f32[16,3,64,128]{3,2,1,0:T(8,128)}), f32[16,3,64,128]{3,2,1,0:T(8,128)S(1)}, u32[]{:S(2)}, u32[]{:S(2)}) async-start(f32[16,3,64,128]{3,2,1,0:T(8,128)} %bitcast.6), calls=%async_computation.3 | async-start | bytes 3145728 | tf_op jit(solution)/shard_map/all_to_all | solution.py:363
  76.9 1.9 copy-start.14
  103.0 1.1 copy-start.9
  112.9 1.2 copy-start.7
  114.1 41.1 %all-to-all-start.2 = ((f32[16,3,64,128]{3,2,1,0:T(8,128)}), f32[16,3,64,128]{3,2,1,0:T(8,128)S(1)}, u32[]{:S(2)}, u32[]{:S(2)}) async-start(f32[16,3,64,128]{3,2,1,0:T(8,128)} %copy-done.9), calls=%async_computation.2 | async-start | bytes 3145728 | tf_op jit(solution)/shard_map/all_to_all | solution.py:384
  119.0 1.4 copy-start.8
  120.4 1.9 copy-start.15
  146.1 1.1 copy-start.6
  155.2 51.3 %all-to-all-start.4 = ((f32[16,3,64,128]{3,2,1,0:T(8,128)}), f32[16,3,64,128]{3,2,1,0:T(8,128)}, u32[]{:S(2)}, u32[]{:S(2)}) async-start(f32[16,3,64,128]{3,2,1,0:T(8,128)} %copy-done.6), calls=%async_computation.4 | async-start | bytes 3145728 | tf_op jit(solution)/shard_map/all_to_all | solution.py:384
  162.1 36.8 %collective-permute-start.1 = (f32[2,8,6144]{2,1,0:T(8,128)}, f32[2,8,6144]{2,1,0:T(8,128)S(1)}, u32[]{:S(2)}, u32[]{:S(2)}) collective-permute-start(f32[2,8,6144]{2,1,0:T(8,128)} %get-tuple-element.5), channel_id=1, source_target_pairs={{0,1},{1,2},{2,3},{3,4},{4,5},{5,6},{6,7},{7,8},{8,9},{9,10},{10,1... | collective-permute-start | bytes 1179656 | tf_op jit(solution)/shard_map/ppermute | solution.py:73
  165.5 35.0 %collective-permute-start.2 = (f32[2,8,6144]{2,1,0:T(8,128)}, f32[2,8,6144]{2,1,0:T(8,128)}, u32[]{:S(2)}, u32[]{:S(2)}) collective-permute-start(f32[2,8,6144]{2,1,0:T(8,128)} %get-tuple-element.4), channel_id=1, source_target_pairs={{1,0},{2,1},{3,2},{4,3},{5,4},{6,5},{7,6},{8,7},{9,8},{10,9},{11,1... | collective-permute-start | bytes 1179656 | tf_op jit(solution)/shard_map/ppermute | solution.py:74
  200.5 1.9 copy-start.3
  206.5 1.0 copy-start.10
  207.6 1.0 copy-start.11
